TPU v7x, 32 devices: a whole 2x2x4 slice. The times are simulated.
32 devices in a mesh: dp: 4 (over y, x), seq: 8 (over z, core).
Axes of the slice: x: 2, y: 2, z: 4, core: 2. Of those that a mesh axis runs over, the one named last changes fastest.
Arguments:
- queries: bfloat16 [4, 1024, 4096], P('dp', 'seq'), may hold values from -6 to 6
- key_states: bfloat16 [4, 1024, 1024], P('dp', 'seq'), may hold values from -8 to 8
- value_states: bfloat16 [4, 1024, 1024], P('dp', 'seq'), may hold values from -6 to 6
- sink_logit: float32 [32], P('seq'), may hold values from 7 to 12
- out_grad: bfloat16 [4, 1024, 4096], P('dp', 'seq'), may hold values from -16 to 16
- block_table: int32 [32, 8, 8], P('seq'), may hold values from 0 to 7, as said below
Outputs:
- query_grad: bfloat16 [4, 1024, 4096], P('dp', 'seq')
- key_grad: bfloat16 [4, 1024, 1024], P('dp', 'seq')
- value_grad: bfloat16 [4, 1024, 1024], P('dp', 'seq')
- sink_grad: float32 [32], P('seq')
Inputs may be any that keep to these rules, and one draw needn't show every extreme that they name: `block_table`: each row lists 8 different key blocks; among them are the query's own block, the two blocks beside it (cyclically) and block 0.
All inputs are finite; a program needn't handle non-finite values.
Results may differ from a plain program's by a relative error of at most 0.0066.
Values may be sent and summed in bfloat16 or wider, within the bound.
A program may use at most 64 MiB of HBM per device.

v0:
```python
import jax
import jax.numpy as jnp
from jax import lax
from jax.sharding import PartitionSpec as P

HEADS = 32
KV_HEADS = 8
HEAD_DIM = 128
BLOCK = 128
KB = 8


def shards(queries, key_states, value_states, sink_logit, out_grad, block_table):
    devices = lax.axis_size("seq")
    tokens_here = queries.shape[1]
    length = tokens_here * devices
    heads_here = HEADS // devices
    group = HEADS // KV_HEADS
    repeats = devices // KV_HEADS
    blocks = length // BLOCK
    scale = HEAD_DIM ** (-0.5)
    key_wide = jnp.repeat(key_states.reshape(1, tokens_here, KV_HEADS, 1, HEAD_DIM), group, axis=3)
    key_wide = key_wide.reshape(1, tokens_here, HEADS * HEAD_DIM)
    value_wide = jnp.repeat(
        value_states.reshape(1, tokens_here, KV_HEADS, 1, HEAD_DIM), group, axis=3
    )
    value_wide = value_wide.reshape(1, tokens_here, HEADS * HEAD_DIM)
    query_all, grad_all, key_all, value_all = (
        lax.all_to_all(queries, "seq", split_axis=2, concat_axis=1, tiled=True),
        lax.all_to_all(out_grad, "seq", split_axis=2, concat_axis=1, tiled=True),
        lax.all_to_all(key_wide, "seq", split_axis=2, concat_axis=1, tiled=True),
        lax.all_to_all(value_wide, "seq", split_axis=2, concat_axis=1, tiled=True),
    )
    key_rows = key_all[0, :, :HEAD_DIM]
    value_rows = value_all[0, :, :HEAD_DIM]
    group_blocks = max(4, blocks // 8)
    step_count = blocks // group_blocks
    query_steps = query_all.reshape(step_count, group_blocks, BLOCK, heads_here, HEAD_DIM)
    grad_steps = grad_all.reshape(step_count, group_blocks, BLOCK, heads_here, HEAD_DIM)
    table_steps = block_table.reshape(heads_here, step_count, group_blocks, KB).transpose(
        1, 0, 2, 3
    )
    key_table = key_rows.reshape(blocks, BLOCK, HEAD_DIM)
    value_table = value_rows.reshape(blocks, BLOCK, HEAD_DIM)
    sink_column = sink_logit[:, None, None]

    def advance(carry, items):
        key_acc, value_acc, sink_acc = carry
        query_group, grad_group, table_group = items
        key_pick = key_table[table_group].reshape(heads_here, group_blocks, KB * BLOCK, HEAD_DIM)
        value_pick = value_table[table_group].reshape(
            heads_here, group_blocks, KB * BLOCK, HEAD_DIM
        )
        scores = (
            jnp.einsum("gqhd,hgkd->hgqk", query_group, key_pick, preferred_element_type=jnp.float32)
            * scale
        )
        top = jnp.maximum(jnp.max(scores, -1), sink_column)
        weights = jnp.exp(scores - top[..., None])
        sink_weight = jnp.exp(sink_column - top)
        total = jnp.sum(weights, -1) + sink_weight
        probs = weights / total[..., None]
        sink_prob = sink_weight / total
        probs_low = probs.astype(jnp.bfloat16)
        attended = jnp.einsum(
            "hgqk,hgkd->gqhd", probs_low, value_pick, preferred_element_type=jnp.float32
        )
        delta_rows = jnp.sum(grad_group.astype(jnp.float32) * attended, -1)
        delta = jnp.transpose(delta_rows, (2, 0, 1))
        dprobs = jnp.einsum(
            "gqhd,hgkd->hgqk", grad_group, value_pick, preferred_element_type=jnp.float32
        )
        dscores = (probs * (dprobs - delta[..., None])).astype(jnp.bfloat16)
        query_part = (
            jnp.einsum("hgqk,hgkd->gqhd", dscores, key_pick, preferred_element_type=jnp.float32)
            * scale
        ).astype(jnp.bfloat16)
        key_terms = (
            jnp.einsum("hgqk,gqhd->hgkd", dscores, query_group, preferred_element_type=jnp.float32)
            * scale
        )
        value_terms = jnp.einsum(
            "hgqk,gqhd->hgkd", probs_low, grad_group, preferred_element_type=jnp.float32
        )
        flat_table = table_group.reshape(-1)
        key_acc = key_acc.at[flat_table].add(
            key_terms.reshape(heads_here * group_blocks * KB, BLOCK, HEAD_DIM)
        )
        value_acc = value_acc.at[flat_table].add(
            value_terms.reshape(heads_here * group_blocks * KB, BLOCK, HEAD_DIM)
        )
        sink_acc = sink_acc - jnp.sum(sink_prob * delta, axis=(1, 2))
        return ((key_acc, value_acc, sink_acc), query_part)

    start = (
        jnp.zeros((blocks, BLOCK, HEAD_DIM), jnp.float32),
        jnp.zeros((blocks, BLOCK, HEAD_DIM), jnp.float32),
        jnp.zeros((heads_here,), jnp.float32),
    )
    finished, query_parts = lax.scan(advance, start, (query_steps, grad_steps, table_steps))
    key_acc, value_acc, sink_acc = finished
    query_local = query_parts.reshape(1, length, heads_here * HEAD_DIM)
    query_grad = lax.all_to_all(query_local, "seq", split_axis=1, concat_axis=2, tiled=True)
    kv_terms = jnp.stack(
        [key_acc.reshape(length, HEAD_DIM), value_acc.reshape(length, HEAD_DIM)], 0
    )
    returned = lax.all_to_all(kv_terms, "seq", split_axis=1, concat_axis=2, tiled=True)
    kv_back = returned.reshape(2, tokens_here, KV_HEADS, repeats, HEAD_DIM).sum(3)
    kv_back = kv_back.reshape(2, tokens_here, KV_HEADS * HEAD_DIM)
    key_grad = kv_back[0:1].astype(jnp.bfloat16)
    value_grad = kv_back[1:2].astype(jnp.bfloat16)
    sink_grad = lax.psum(sink_acc, "dp")
    return (query_grad, key_grad, value_grad, sink_grad)


def solution(mesh):
    in_specs = (
        P("dp", "seq", None),
        P("dp", "seq", None),
        P("dp", "seq", None),
        P("seq"),
        P("dp", "seq", None),
        P("seq", None, None),
    )
    out_specs = (P("dp", "seq", None), P("dp", "seq", None), P("dp", "seq", None), P("seq"))
    return jax.shard_map(shards, mesh=mesh, in_specs=in_specs, out_specs=out_specs, check_vma=False)
```

profile of v0, /device:TPU:0, one launch (start us, length us, event | category | flops | bytes accessed | tf_op | source)
XLA Modules:
  0.0 403.6 jit_solution(6500077829223670325)
XLA Ops:
  2.0 16.7 %copy.143 = bf16[1,128,4096]{1,0,2:T(2,128)(2,1)S(1)} copy(bf16[1,128,4096]{1,2,0:T(8,128)(2,1)S(1)} %bitcast.160) | data formatting | bytes 2097152 | tf_op jit(solution)/shard_map/broadcast_in_dim | solution.py:22
  19.3 22.4 %reduce.1 = bf16[4096,128]{1,0:T(8,128)(2,1)S(1)} reduce(bf16[4096,1,128]{2,1,0:T(2,128)(2,1)S(1)} %bitcast.155, bf16[]{:T(256)} %broadcast.115), dimensions={1}, to_apply=%bitcast.95.reduce_sub_computation | reduce | bytes 2097154
  42.8 6.3 %all-to-all-start.1 = ((bf16[8,2,32768]{2,1,0:T(2,128)(2,1)}), bf16[8,2,32768]{2,1,0:T(2,128)(2,1)S(1)}, u32[]{:S(2)}, u32[]{:S(2)}) async-start(bf16[8,2,32768]{2,1,0:T(2,128)(2,1)} %reshape.218), calls=%async_computation.1 | async-start | bytes 2097152 | tf_op jit(solution)/shard_map/all_to_all | solution.py:31
  49.6 16.7 %copy.142 = bf16[1,128,4096]{1,0,2:T(2,128)(2,1)S(1)} copy(bf16[1,128,4096]{1,2,0:T(8,128)(2,1)S(1)} %bitcast.161) | data formatting | bytes 2097152 | tf_op jit(solution)/shard_map/broadcast_in_dim | solution.py:24
  66.3 23.4 %reduce.3 = bf16[4096,128]{1,0:T(8,128)(2,1)} reduce(bf16[4096,1,128]{2,1,0:T(2,128)(2,1)S(1)} %bitcast.157, bf16[]{:T(256)} %broadcast.115), dimensions={1}, to_apply=%bitcast.94.reduce_sub_computation | reduce | bytes 2097154
  91.9 5.1 %all-to-all-start.3 = ((bf16[8,2,32768]{2,1,0:T(2,128)(2,1)}), bf16[8,2,32768]{2,1,0:T(2,128)(2,1)}, u32[]{:S(2)}, u32[]{:S(2)}) async-start(bf16[8,2,32768]{2,1,0:T(2,128)(2,1)} %reshape.222), calls=%async_computation.3 | async-start | bytes 2097152 | tf_op jit(solution)/shard_map/all_to_all | solution.py:32
  97.0 5.0 %copy.84 = bf16[1,128,4096]{1,0,2:T(2,128)(2,1)S(1)} copy(bf16[1,128,4096]{2,1,0:T(8,128)(2,1)} %param.8) | data formatting | bytes 2097152 | tf_op args[0]
  102.0 23.4 %reduce = bf16[4096,128]{1,0:T(8,128)(2,1)} reduce(bf16[4096,1,128]{2,1,0:T(2,128)(2,1)S(1)} %bitcast.158, bf16[]{:T(256)} %broadcast.115), dimensions={1}, to_apply=%bitcast.76.reduce_sub_computation | reduce | bytes 2097154
  127.5 5.1 %all-to-all-start = ((bf16[8,2,32768]{2,1,0:T(2,128)(2,1)}), bf16[8,2,32768]{2,1,0:T(2,128)(2,1)}, u32[]{:S(2)}, u32[]{:S(2)}) async-start(bf16[8,2,32768]{2,1,0:T(2,128)(2,1)} %reshape.216), calls=%async_computation | async-start | bytes 2097152 | tf_op jit(solution)/shard_map/all_to_all | solution.py:29
  132.6 5.0 %copy.88 = bf16[1,128,4096]{1,0,2:T(2,128)(2,1)S(1)} copy(bf16[1,128,4096]{2,1,0:T(8,128)(2,1)} %param.12) | data formatting | bytes 2097152 | tf_op args[4]
  137.7 23.4 %reduce.2 = bf16[4096,128]{1,0:T(8,128)(2,1)} reduce(bf16[4096,1,128]{2,1,0:T(2,128)(2,1)S(1)} %bitcast.159, bf16[]{:T(256)} %broadcast.115), dimensions={1}, to_apply=%bitcast.80.reduce_sub_computation | reduce | bytes 2097154
  163.2 5.1 %all-to-all-start.2 = ((bf16[8,2,32768]{2,1,0:T(2,128)(2,1)}), bf16[8,2,32768]{2,1,0:T(2,128)(2,1)}, u32[]{:S(2)}, u32[]{:S(2)}) async-start(bf16[8,2,32768]{2,1,0:T(2,128)(2,1)} %reshape.220), calls=%async_computation.2 | async-start | bytes 2097152 | tf_op jit(solution)/shard_map/all_to_all | solution.py:30
  170.1 4.3 %reshape.223 = bf16[4096,1,128]{2,1,0:T(2,128)(2,1)S(1)} reshape(bf16[8,2,32768]{2,1,0:T(2,128)(2,1)} %all-to-all-done.3) | data formatting | bytes 2097152
  175.2 4.3 %reshape.217 = bf16[4096,1,128]{2,1,0:T(2,128)(2,1)S(1)} reshape(bf16[8,2,32768]{2,1,0:T(2,128)(2,1)} %all-to-all-done) | data formatting | bytes 2097152
  180.7 14.3 %all-to-all-done.2 = bf16[8,2,32768]{2,1,0:T(2,128)(2,1)} async-done(((bf16[8,2,32768]{2,1,0:T(2,128)(2,1)}), bf16[8,2,32768]{2,1,0:T(2,128)(2,1)}, u32[]{:S(2)}, u32[]{:S(2)}) %all-to-all-start.2) | async-done | bytes 1048608 | tf_op jit(solution)/shard_map/all_to_all | solution.py:30
  195.0 4.3 %reshape.221 = bf16[4096,1,128]{2,1,0:T(2,128)(2,1)S(1)} reshape(bf16[8,2,32768]{2,1,0:T(2,128)(2,1)} %all-to-all-done.2) | data formatting | bytes 2097152
  200.6 147.5 %while.17 = (s32[]{:T(128)}, f32[8,128,128]{2,1,0:T(8,128)S(1)}, f32[8,128,128]{2,1,0:T(8,128)S(1)}, f32[4]{0:T(128)S(1)}, bf16[2,4,128,4,128]{4,3,2,1,0:T(4,128...) while((s32[]{:T(128)}, f32[8,128,128]{2,1,0:T(8,128)S(1)}, ...), condition=%wide.region_7.8_spmd.clone, body=%wide.region_0.7_spmd.clone.sunk | while | flops 3268689664 | bytes 217223056 | solution.py:100
  217.8 3.5 multiply_reduce_fusion.4
  231.8 4.8 %fusion.81 = f32[4,4,1024,128]{3,2,1,0:T(8,128)} fusion(bf16[1,4,128,4,128]{4,2,1,3,0:T(8,128)(2,1)S(1)} %copy.151, f32[4,4,128,1024]{3,2,1,0:T(8,128)S(1)} %get-tuple-element.261, f32[4,4,128]{2,1,0:T(4,128)S(1)} %fusion.79, f32[4,4,128]{2,1,0:T(4,128)S(1)} %broadcast_maximum_fusion.2), kind=kOutput, calls=%fused_computation.13.clone.1 | convolution fusion | flops 545259520 | bytes 17317888 | tf_op jit(solution)/shard_map/while/body/eval_jaxpr/hgqk,gqhd->hgkd/dot_general | solution.py:82
  236.5 17.0 %scatter_fusion.1 = f32[8,128,128]{2,1,0:T(8,128)S(1)} fusion(f32[8,128,128]{2,1,0:T(8,128)S(1)} %get-tuple-element.278, s32[128]{0:T(128)S(1)} %fusion.77, f32[128,128,128]{2,1,0:T(8,128)} %bitcast.145), kind=kCustom, calls=%fused_computation.3.clone.clone.1 | custom fusion | flops 2097152 | bytes 25166336 | tf_op jit(solution)/shard_map/while/body/eval_jaxpr/scatter-add | solution.py:89
  254.9 6.8 %broadcast_multiply_fusion.2 = f32[4,4,1024,128]{3,2,1,0:T(8,128)} fusion(bf16[4,4,128,1024]{3,2,1,0:T(8,128)(2,1)} %copy-done.1, bf16[1,4,128,4,128]{4,2,1,3,0:T(8,128)(2,1)S(1)} %copy.152), kind=kOutput, calls=%fused_computation.12.clone.1 | convolution fusion | flops 538968064 | bytes 13107200 | tf_op jit(solution)/shard_map/while/body/eval_jaxpr/hgqk,gqhd->hgkd/dot_general | solution.py:79
  261.7 17.0 %scatter_fusion = f32[8,128,128]{2,1,0:T(8,128)S(1)} fusion(f32[8,128,128]{2,1,0:T(8,128)S(1)} %get-tuple-element.277, s32[128]{0:T(128)S(1)} %fusion.77, f32[128,128,128]{2,1,0:T(8,128)} %bitcast.142), kind=kCustom, calls=%fused_computation.2.clone.clone.1 | custom fusion | flops 2097152 | bytes 25166336 | tf_op jit(solution)/shard_map/while/body/eval_jaxpr/scatter-add | solution.py:86
  300.9 4.8 %fusion.81 = f32[4,4,1024,128]{3,2,1,0:T(8,128)} fusion(bf16[1,4,128,4,128]{4,2,1,3,0:T(8,128)(2,1)S(1)} %copy.151, f32[4,4,128,1024]{3,2,1,0:T(8,128)S(1)} %get-tuple-element.261, f32[4,4,128]{2,1,0:T(4,128)S(1)} %fusion.79, f32[4,4,128]{2,1,0:T(4,128)S(1)} %broadcast_maximum_fusion.2), kind=kOutput, calls=%fused_computation.13.clone.1 | convolution fusion | flops 545259520 | bytes 17317888 | tf_op jit(solution)/shard_map/while/body/eval_jaxpr/hgqk,gqhd->hgkd/dot_general | solution.py:82
  305.6 17.0 %scatter_fusion.1 = f32[8,128,128]{2,1,0:T(8,128)S(1)} fusion(f32[8,128,128]{2,1,0:T(8,128)S(1)} %get-tuple-element.278, s32[128]{0:T(128)S(1)} %fusion.77, f32[128,128,128]{2,1,0:T(8,128)} %bitcast.145), kind=kCustom, calls=%fused_computation.3.clone.clone.1 | custom fusion | flops 2097152 | bytes 25166336 | tf_op jit(solution)/shard_map/while/body/eval_jaxpr/scatter-add | solution.py:89
  324.0 6.8 %broadcast_multiply_fusion.2 = f32[4,4,1024,128]{3,2,1,0:T(8,128)} fusion(bf16[4,4,128,1024]{3,2,1,0:T(8,128)(2,1)} %copy-done.1, bf16[1,4,128,4,128]{4,2,1,3,0:T(8,128)(2,1)S(1)} %copy.152), kind=kOutput, calls=%fused_computation.12.clone.1 | convolution fusion | flops 538968064 | bytes 13107200 | tf_op jit(solution)/shard_map/while/body/eval_jaxpr/hgqk,gqhd->hgkd/dot_general | solution.py:79
  330.8 17.0 %scatter_fusion = f32[8,128,128]{2,1,0:T(8,128)S(1)} fusion(f32[8,128,128]{2,1,0:T(8,128)S(1)} %get-tuple-element.277, s32[128]{0:T(128)S(1)} %fusion.77, f32[128,128,128]{2,1,0:T(8,128)} %bitcast.142), kind=kCustom, calls=%fused_computation.2.clone.clone.1 | custom fusion | flops 2097152 | bytes 25166336 | tf_op jit(solution)/shard_map/while/body/eval_jaxpr/scatter-add | solution.py:86
  349.8 4.1 %all-to-all-start.5 = ((bf16[2,1024,128]{2,0,1:T(2,128)(2,1)}), bf16[2,1024,128]{2,0,1:T(2,128)(2,1)}, u32[]{:S(2)}, u32[]{:S(2)}) async-start(bf16[2,1024,128]{2,0,1:T(2,128)(2,1)} %pad_maximum_fusion), calls=%async_computation.5 | async-start | bytes 1048576 | tf_op jit(solution)/shard_map/all_to_all | solution.py:107
  353.9 5.9 %reshape.215 = bf16[1,1024,512]{2,0,1:T(2,128)(2,1)S(1)} reshape(bf16[2,4,128,4,128]{4,3,2,1,0:T(4,128)(2,1)} %get-tuple-element.64) | data formatting | bytes 2097152 | tf_op jit(solution)/shard_map/reshape | solution.py:102
  359.8 7.0 %reduce.4 = bf16[1024,512]{1,0:T(8,128)(2,1)S(1)} reduce(bf16[1024,1,512]{2,1,0:T(2,128)(2,1)S(1)} %bitcast.156, bf16[]{:T(256)} %broadcast.115), dimensions={1}, to_apply=%bitcast.84.reduce_sub_computation | reduce | bytes 2097154
  369.3 4.1 %all-to-all-start.4 = ((bf16[8,2,32768]{2,1,0:T(2,128)(2,1)}), bf16[8,2,32768]{2,1,0:T(2,128)(2,1)S(1)}, u32[]{:S(2)}, u32[]{:S(2)}) async-start(bf16[8,2,32768]{2,1,0:T(2,128)(2,1)} %reshape.224), calls=%async_computation.4 | async-start | bytes 2097152 | tf_op jit(solution)/shard_map/all_to_all | solution.py:103
  373.4 10.4 %psum.7 = f32[4]{0:T(128)} all-reduce(f32[4]{0:T(128)S(1)} %get-tuple-element.67), channel_id=1, replica_groups=mesh['dp'=4,'seq'=8] {'dp'}, use_global_device_ids=true, to_apply=%region_8.9 | all-reduce | flops 4 | bytes 32 | tf_op jit(solution)/shard_map/psum | solution.py:112
  387.1 13.0 %all-to-all-done.4 = bf16[8,2,32768]{2,1,0:T(2,128)(2,1)S(1)} async-done(((bf16[8,2,32768]{2,1,0:T(2,128)(2,1)}), bf16[8,2,32768]{2,1,0:T(2,128)(2,1)S(1)}, u32[]{:S(2)}, u32[]{:S(2)}) %all-to-all-start.4) | async-done | bytes 1048608 | tf_op jit(solution)/shard_map/all_to_all | solution.py:103
  (103 shorter events, 68.7 us)
Async XLA Ops:
  0.6 48.5 %copy-start.5 = (bf16[1,128,1024]{2,1,0:T(8,128)(2,1)S(1)}, bf16[1,128,1024]{2,1,0:T(8,128)(2,1)}, u32[]{:S(2)}) copy-start(bf16[1,128,1024]{2,1,0:T(8,128)(2,1)} %param.10) | copy-start | bytes 786436
  42.8 49.1 %all-to-all-start.1 = ((bf16[8,2,32768]{2,1,0:T(2,128)(2,1)}), bf16[8,2,32768]{2,1,0:T(2,128)(2,1)S(1)}, u32[]{:S(2)}, u32[]{:S(2)}) async-start(bf16[8,2,32768]{2,1,0:T(2,128)(2,1)} %reshape.218), calls=%async_computation.1 | async-start | bytes 2097152 | tf_op jit(solution)/shard_map/all_to_all | solution.py:31
  91.9 35.6 %all-to-all-start.3 = ((bf16[8,2,32768]{2,1,0:T(2,128)(2,1)}), bf16[8,2,32768]{2,1,0:T(2,128)(2,1)}, u32[]{:S(2)}, u32[]{:S(2)}) async-start(bf16[8,2,32768]{2,1,0:T(2,128)(2,1)} %reshape.222), calls=%async_computation.3 | async-start | bytes 2097152 | tf_op jit(solution)/shard_map/all_to_all | solution.py:32
  127.5 35.7 %all-to-all-start = ((bf16[8,2,32768]{2,1,0:T(2,128)(2,1)}), bf16[8,2,32768]{2,1,0:T(2,128)(2,1)}, u32[]{:S(2)}, u32[]{:S(2)}) async-start(bf16[8,2,32768]{2,1,0:T(2,128)(2,1)} %reshape.216), calls=%async_computation | async-start | bytes 2097152 | tf_op jit(solution)/shard_map/all_to_all | solution.py:29
  163.2 31.8 %all-to-all-start.2 = ((bf16[8,2,32768]{2,1,0:T(2,128)(2,1)}), bf16[8,2,32768]{2,1,0:T(2,128)(2,1)}, u32[]{:S(2)}, u32[]{:S(2)}) async-start(bf16[8,2,32768]{2,1,0:T(2,128)(2,1)} %reshape.220), calls=%async_computation.2 | async-start | bytes 2097152 | tf_op jit(solution)/shard_map/all_to_all | solution.py:30
  174.6 26.0 %copy-start.4 = (s32[4,8,8]{2,1,0:T(8,128)S(1)}, s32[4,8,8]{2,1,0:T(8,128)}, u32[]{:S(2)}) copy-start(s32[4,8,8]{2,1,0:T(8,128)} %param.13) | copy-start | bytes 3076
  174.6 25.9 %copy-start.6 = (f32[4]{0:T(128)S(1)}, f32[4]{0:T(128)}, u32[]{:S(2)}) copy-start(f32[4]{0:T(128)} %param.11) | copy-start | bytes 52
  221.3 2.2 copy-start.2
  226.4 2.9 copy-start
  229.2 7.3 %copy-start.1 = (bf16[4,4,128,1024]{3,2,1,0:T(8,128)(2,1)}, bf16[4,4,128,1024]{3,2,1,0:T(8,128)(2,1)S(1)}, u32[]{:S(2)}) copy-start(bf16[4,4,128,1024]{3,2,1,0:T(8,128)(2,1)S(1)} %multiply_convert_fusion.2) | copy-start | bytes 12582916 | tf_op jit(solution)/shard_map/while
  236.5 17.0 %copy-start.3 = (bf16[1,4,128,4,128]{2,4,3,1,0:T(8,128)(2,1)S(1)}, bf16[1,4,128,4,128]{2,4,3,1,0:T(8,128)(2,1)}, u32[]{:S(2)}) copy-start(bf16[1,4,128,4,128]{2,4,3,1,0:T(8,128)(2,1)} %fusion.83) | copy-start | bytes 1572868 | tf_op jit(solution)/shard_map/while
  290.4 2.2 copy-start.2
  295.5 2.8 copy-start
  298.3 7.3 %copy-start.1 = (bf16[4,4,128,1024]{3,2,1,0:T(8,128)(2,1)}, bf16[4,4,128,1024]{3,2,1,0:T(8,128)(2,1)S(1)}, u32[]{:S(2)}) copy-start(bf16[4,4,128,1024]{3,2,1,0:T(8,128)(2,1)S(1)} %multiply_convert_fusion.2) | copy-start | bytes 12582916 | tf_op jit(solution)/shard_map/while
  305.6 17.0 %copy-start.3 = (bf16[1,4,128,4,128]{2,4,3,1,0:T(8,128)(2,1)S(1)}, bf16[1,4,128,4,128]{2,4,3,1,0:T(8,128)(2,1)}, u32[]{:S(2)}) copy-start(bf16[1,4,128,4,128]{2,4,3,1,0:T(8,128)(2,1)} %fusion.83) | copy-start | bytes 1572868 | tf_op jit(solution)/shard_map/while
  349.8 19.5 %all-to-all-start.5 = ((bf16[2,1024,128]{2,0,1:T(2,128)(2,1)}), bf16[2,1024,128]{2,0,1:T(2,128)(2,1)}, u32[]{:S(2)}, u32[]{:S(2)}) async-start(bf16[2,1024,128]{2,0,1:T(2,128)(2,1)} %pad_maximum_fusion), calls=%async_computation.5 | async-start | bytes 1048576 | tf_op jit(solution)/shard_map/all_to_all | solution.py:107
  369.3 30.7 %all-to-all-start.4 = ((bf16[8,2,32768]{2,1,0:T(2,128)(2,1)}), bf16[8,2,32768]{2,1,0:T(2,128)(2,1)S(1)}, u32[]{:S(2)}, u32[]{:S(2)}) async-start(bf16[8,2,32768]{2,1,0:T(2,128)(2,1)} %reshape.224), calls=%async_computation.4 | async-start | bytes 2097152 | tf_op jit(solution)/shard_map/all_to_all | solution.py:103
where the time goes:
time: 410 us; the launch traced here: 404 us
  other arithmetic  174 us (42%)
  local copies, waits for them, and re-layouts  104 us (25%)
  matrix products  46.2 us (11%)
  starting transfers between devices  29.9 us (7%)
  waiting for transfers between devices  28.2 us (7%)
  blocking collectives  10.4 us (3%)
  loops' own time  9.54 us (2%)
    unnamed x6, other arithmetic  99.6 us
    unnamed x27, local copies, waits for them, and re-layouts  40.7 us
    scatter-add x2, other arithmetic, advance(): value_acc.at[flat_table]  34 us
    scatter-add x2, other arithmetic, advance(): key_acc.at[flat_table]  34 us
    broadcast_in_dim x2, local copies, waits for them, and re-layouts, shards(): jnp.repeat(value_states.reshape(1, tokens_here, KV_HEADS, 1, HEAD_DIM), g...  17 us
    broadcast_in_dim x2, local copies, waits for them, and re-layouts, shards(): jnp.repeat(key_states.reshape(1, tokens_here, KV_HEADS, 1, HEAD_DIM), gro...  17 us
    all_to_all x1, waiting for transfers between devices, shards(): lax.all_to_all(out_grad, 'seq', split_axis=2, concat_axis=1, tiled=True)  14.3 us
    dot_general x2, matrix products, advance(): jnp.einsum('hgqk,gqhd->hgkd', dscores, query_group, preferred_element_typ...  13.6 us
  transfers between devices with their start and end apart: 6, of which 3 were waited for; matrix products, arithmetic and copies ran while one was open for 33% of the time, Pallas kernels for 0%

commit v1 on v0

--- a/solution.py
+++ b/solution.py
@@ -1,6 +1,8 @@
 import jax
 import jax.numpy as jnp
 from jax import lax
+from jax.experimental import pallas as pl
+from jax.experimental.pallas import tpu as pltpu
 from jax.sharding import PartitionSpec as P
 
 HEADS = 32
@@ -10,7 +12,7 @@
 KB = 8
 
 
-def shards(queries, key_states, value_states, sink_logit, out_grad, block_table):
+def sparse_shards(queries, key_states, value_states, sink_logit, out_grad, block_table):
     devices = lax.axis_size("seq")
     tokens_here = queries.shape[1]
     length = tokens_here * devices
@@ -113,6 +115,388 @@
     return (query_grad, key_grad, value_grad, sink_grad)
 
 
+F32 = jnp.float32
+BF16 = jnp.bfloat16
+GROUP = HEADS // KV_HEADS
+SCALE = HEAD_DIM ** (-0.5)
+
+
+def group_terms(keys, values, queries, grads, sink_row):
+    nt = (((1,), (1,)), ((), ()))
+    tn = (((0,), (0,)), ((), ()))
+    scores = lax.dot_general(keys, queries, nt, preferred_element_type=F32) * SCALE
+    dprobs = lax.dot_general(values, grads, nt, preferred_element_type=F32)
+    top = jnp.maximum(jnp.max(scores, 0, keepdims=True), sink_row)
+    weights = jnp.exp(scores - top)
+    sink_weight = jnp.exp(sink_row - top)
+    inverse = 1.0 / (jnp.sum(weights, 0, keepdims=True) + sink_weight)
+    probs = weights * inverse
+    probs_low = probs.astype(BF16)
+    delta = jnp.sum(probs_low.astype(F32) * dprobs, 0, keepdims=True)
+    dscores = (probs * (dprobs - delta)).astype(BF16)
+    value_terms = jnp.dot(probs_low, grads, preferred_element_type=F32)
+    key_terms = jnp.dot(dscores, queries, preferred_element_type=F32)
+    query_terms = lax.dot_general(keys, dscores, tn, preferred_element_type=F32)
+    return key_terms, value_terms, query_terms.T * SCALE, -(sink_weight * inverse) * delta
+
+
+def dense_kernel(
+    q_ref, g_ref, k_ref, v_ref, sink_ref,
+    dq_ref, dk_ref, dv_ref, ds_ref,
+    kv_all, acc, part, pair_out, pair_in, right_out, right_in, left_out, left_in,
+    sink_all, sink_part, sink_in, sink_dp,
+    right_s, right_r, left_s, left_r, sib_s, sib_r, pair_s, pair_r,
+    sumr_s, sumr_r, suml_s, suml_r, logit_s, logit_r, sg_s, sg_r, dp_s, dp_r,
+):
+    devices = lax.axis_size("seq")
+    chips = devices // 2
+    last = chips - 1
+    dps = lax.axis_size("dp")
+    me = lax.axis_index("seq")
+    my_dp = lax.axis_index("dp")
+    chip = lax.div(me, 2)
+    lane = lax.rem(me, 2)
+    sibling = me + 1 - 2 * lane
+    here = HEAD_DIM
+    wide = GROUP * HEAD_DIM
+
+    def remote(src, dst, send_sem, recv_sem, **target):
+        return pltpu.make_async_remote_copy(
+            src_ref=src, dst_ref=dst, send_sem=send_sem, recv_sem=recv_sem,
+            device_id=target, device_id_type=pl.DeviceIdType.MESH,
+        )
+
+    def shard(h, z, which):
+        return kv_all.at[:, h, 2 * z + which]
+
+    def go_right(h, k, z):
+        ref = shard(h, z, lane)
+        return remote(ref, ref, right_s.at[h, k], right_r.at[h, k], seq=me + 2)
+
+    def go_left(h, k, z):
+        ref = shard(h, z, lane)
+        return remote(ref, ref, left_s.at[h, k], left_r.at[h, k], seq=me - 2)
+
+    def go_across(h, z, which):
+        ref = shard(h, z, which)
+        return remote(ref, ref, sib_s.at[h, z], sib_r.at[h, z], seq=sibling)
+
+    def go_pair(h):
+        return remote(pair_out.at[h], pair_in.at[h], pair_s.at[h], pair_r.at[h], seq=sibling)
+
+    def sum_right(h, d):
+        return remote(
+            right_out.at[h, d], right_in.at[h, d], sumr_s.at[h, d], sumr_r.at[h, d], seq=me + 2
+        )
+
+    def sum_left(h, d):
+        return remote(
+            left_out.at[h, d], left_in.at[h, d], suml_s.at[h, d], suml_r.at[h, d], seq=me - 2
+        )
+
+    def logit(i, owner):
+        ref = sink_all.at[owner]
+        return remote(ref, ref, logit_s.at[i], logit_r.at[i], seq=lax.rem(me + i, devices))
+
+    def sink_send(h):
+        return remote(sink_part.at[h], sink_in.at[me], sg_s.at[h], sg_r.at[me], seq=h)
+
+    def sink_recv(p):
+        return remote(sink_part.at[p], sink_in.at[p], sg_s.at[p], sg_r.at[p], seq=p)
+
+    def across_dp(i, owner):
+        ref = sink_dp.at[owner]
+        return remote(ref, ref, dp_s.at[i], dp_r.at[i], dp=lax.rem(my_dp + i, dps))
+
+    barrier = pltpu.get_barrier_semaphore()
+    for i in range(1, devices):
+        pl.semaphore_signal(
+            barrier, inc=1, device_id={"seq": lax.rem(me + i, devices)},
+            device_id_type=pl.DeviceIdType.MESH,
+        )
+    for i in range(1, dps):
+        pl.semaphore_signal(
+            barrier, inc=1, device_id={"dp": lax.rem(my_dp + i, dps)},
+            device_id_type=pl.DeviceIdType.MESH,
+        )
+
+    for h in range(KV_HEADS):
+        cut = slice(h * HEAD_DIM, (h + 1) * HEAD_DIM)
+        kv_all[0, h, me] = k_ref[:, cut]
+        kv_all[1, h, me] = v_ref[:, cut]
+    sink_all[me] = sink_ref[...]
+    sink_part[...] = jnp.zeros_like(sink_part)
+    pl.semaphore_wait(barrier, devices - 1 + dps - 1)
+
+    def send_own(h):
+        @pl.when(chip < last)
+        def _():
+            go_right(h, 0, chip).start()
+
+        @pl.when(chip > 0)
+        def _():
+            go_left(h, 0, chip).start()
+
+        go_across(h, chip, lane).start()
+
+    send_own(0)
+    for i in range(1, devices):
+        logit(i, me).start()
+    send_own(1)
+    for i in range(1, devices):
+        logit(i, lax.rem(me - i + devices, devices)).wait_recv()
+
+    def hand_on(h, k):
+        @pl.when(chip >= k)
+        def _():
+            go_right(h, k - 1, chip - k).wait_recv()
+            if k < last:
+
+                @pl.when(chip < last)
+                def _():
+                    go_right(h, k, chip - k).start()
+
+            go_across(h, chip - k, lane).start()
+
+        @pl.when(chip + k <= last)
+        def _():
+            go_left(h, k - 1, chip + k).wait_recv()
+            if k < last:
+
+                @pl.when(chip > 0)
+                def _():
+                    go_left(h, k, chip + k).start()
+
+            go_across(h, chip + k, lane).start()
+
+    def compute(h):
+        for z in range(chips):
+            go_across(h, z, 1 - lane).wait_recv()
+        keys = kv_all[0, h].reshape(devices * here, HEAD_DIM)
+        values = kv_all[1, h].reshape(devices * here, HEAD_DIM)
+        key_sum = value_sum = None
+        for half in range(2):
+            heads = range(half * GROUP // 2, (half + 1) * GROUP // 2)
+            cuts = [
+                pl.ds(pl.multiple_of(h * wide + j * HEAD_DIM, HEAD_DIM), HEAD_DIM) for j in heads
+            ]
+            queries = jnp.concatenate([q_ref[:, cut] for cut in cuts], 0)
+            grads = jnp.concatenate([g_ref[:, cut] for cut in cuts], 0)
+            sink_row = jnp.concatenate([sink_all[h, j : j + 1, :] for j in heads], 1)
+            key_terms, value_terms, query_terms, sink_terms = group_terms(
+                keys, values, queries, grads, sink_row
+            )
+            key_sum = key_terms if key_sum is None else key_sum + key_terms
+            value_sum = value_terms if value_sum is None else value_sum + value_terms
+            for i, j in enumerate(heads):
+                span = slice(i * here, (i + 1) * here)
+                dq_ref[:, cuts[i]] = query_terms[span].astype(BF16)
+                sink_part[h, j : j + 1, :] = sink_terms[:, span]
+        acc[0] = (key_sum * SCALE).reshape(devices, here, HEAD_DIM)
+        acc[1] = value_sum.reshape(devices, here, HEAD_DIM)
+        for d in range(chips):
+            pair_out[h, d] = acc[:, 2 * d + 1 - lane].astype(BF16)
+        go_pair(h).start()
+        for d in range(chips):
+            part[h, d] = acc[:, 2 * d + lane]
+
+        @pl.when(h == me)
+        def _():
+            sink_in[me] = sink_part[h]
+
+        @pl.when(h != me)
+        def _():
+            sink_send(h).start()
+
+    def pair_sum(h):
+        go_pair(h).wait_recv()
+        for d in range(chips):
+            part[h, d] = part[h, d] + pair_in[h, d].astype(F32)
+
+    def pass_right(h):
+        for d in range(last, 0, -1):
+
+            @pl.when(d > chip)
+            def _():
+                @pl.when(chip == 0)
+                def _():
+                    right_out[h, d] = part[h, d].astype(BF16)
+
+                @pl.when(chip > 0)
+                def _():
+                    sum_right(h, d).wait_recv()
+                    right_out[h, d] = (part[h, d] + right_in[h, d].astype(F32)).astype(BF16)
+
+                sum_right(h, d).start()
+
+    def pass_left(h):
+        for d in range(last):
+
+            @pl.when(d < chip)
+            def _():
+                @pl.when(chip == last)
+                def _():
+                    left_out[h, d] = part[h, d].astype(BF16)
+
+                @pl.when(chip < last)
+                def _():
+                    sum_left(h, d).wait_recv()
+                    left_out[h, d] = (part[h, d] + left_in[h, d].astype(F32)).astype(BF16)
+
+                sum_left(h, d).start()
+
+    def finish(h):
+        @pl.when(chip > 0)
+        def _():
+            sum_right(h, chip).wait_recv()
+            part[h, chip] = part[h, chip] + right_in[h, chip].astype(F32)
+
+        @pl.when(chip < last)
+        def _():
+            sum_left(h, chip).wait_recv()
+            part[h, chip] = part[h, chip] + left_in[h, chip].astype(F32)
+
+        cut = pl.ds(pl.multiple_of(h * HEAD_DIM, HEAD_DIM), HEAD_DIM)
+        dk_ref[:, cut] = part[h, chip, 0].astype(BF16)
+        dv_ref[:, cut] = part[h, chip, 1].astype(BF16)
+
+    def sink_sum():
+        for p in range(devices):
+
+            @pl.when(p != me)
+            def _():
+                sink_recv(p).wait_recv()
+
+        sink_dp[my_dp] = jnp.sum(sink_in[...], 0)
+        for i in range(1, dps):
+            across_dp(i, my_dp).start()
+
+    def in_range(h):
+        return (h >= 0) & (h < KV_HEADS)
+
+    compute_at = chips
+    pair_at = compute_at + 1
+    finish_at = pair_at + last
+
+    def tick(t, carry):
+        def at(h, step, also=None):
+            ready = in_range(h) if also is None else in_range(h) & also
+
+            @pl.when(ready)
+            def _():
+                step(h)
+
+        at(t + 2, send_own)
+        for k in range(1, chips):
+            at(t - k, lambda h: hand_on(h, k))
+        at(t - pair_at, pair_sum)
+        at(t - pair_at - chip, pass_right, chip < last)
+        at(t - pair_at - (last - chip), pass_left, chip > 0)
+        at(t - compute_at, compute)
+        at(t - finish_at, finish)
+
+        @pl.when(t == compute_at + KV_HEADS + 1)
+        def _():
+            sink_sum()
+
+        return carry
+
+    lax.fori_loop(0, finish_at + KV_HEADS, tick, 0)
+
+    for i in range(1, dps):
+        across_dp(i, lax.rem(my_dp - i + dps, dps)).wait_recv()
+    total = sink_dp[0]
+    for i in range(1, dps):
+        total = total + sink_dp[i]
+    ds_ref[...] = jnp.broadcast_to(jnp.sum(total, 1, keepdims=True), ds_ref.shape)
+
+    def drain(h, carry):
+        for k in range(last):
+
+            @pl.when((chip >= k) & (chip < last))
+            def _():
+                go_right(h, k, chip - k).wait_send()
+
+            @pl.when((chip + k <= last) & (chip > 0))
+            def _():
+                go_left(h, k, chip + k).wait_send()
+
+        for z in range(chips):
+            go_across(h, z, lane).wait_send()
+        go_pair(h).wait_send()
+        for d in range(chips):
+
+            @pl.when(d > chip)
+            def _():
+                sum_right(h, d).wait_send()
+
+            @pl.when(d < chip)
+            def _():
+                sum_left(h, d).wait_send()
+
+        @pl.when(h != me)
+        def _():
+            sink_send(h).wait_send()
+
+        return carry
+
+    lax.fori_loop(0, KV_HEADS, drain, 0)
+    for i in range(1, devices):
+        logit(i, me).wait_send()
+    for i in range(1, dps):
+        across_dp(i, my_dp).wait_send()
+
+
+def dense_shards(queries, key_states, value_states, sink_logit, out_grad, block_table):
+    devices = lax.axis_size("seq")
+    chips = devices // 2
+    dps = lax.axis_size("dp")
+    here = queries.shape[1]
+    tile = (here, HEAD_DIM)
+    sink_tile = jnp.pad(jnp.broadcast_to(sink_logit[:, None], (GROUP, HEAD_DIM)), ((0, 8 - GROUP), (0, 0)))
+    dma = pltpu.SemaphoreType.DMA
+    vmem = pl.BlockSpec(memory_space=pltpu.VMEM)
+    flat = KV_HEADS * HEAD_DIM
+    steps = [(KV_HEADS, chips - 1)] * 4 + [(KV_HEADS, chips)] * 2 + [(KV_HEADS,)] * 2
+    steps += [(KV_HEADS, chips)] * 4 + [(devices,)] * 4 + [(dps,)] * 2
+    per_head = pltpu.VMEM((KV_HEADS, chips, 2) + tile, BF16)
+    query_grad, key_grad, value_grad, sink_sum = pl.pallas_call(
+        dense_kernel,
+        in_specs=[vmem] * 5,
+        out_specs=[vmem] * 4,
+        out_shape=[
+            jax.ShapeDtypeStruct((here, HEADS * HEAD_DIM), BF16),
+            jax.ShapeDtypeStruct((here, flat), BF16),
+            jax.ShapeDtypeStruct((here, flat), BF16),
+            jax.ShapeDtypeStruct((8, HEAD_DIM), F32),
+        ],
+        scratch_shapes=[
+            pltpu.VMEM((2, KV_HEADS, devices) + tile, BF16),
+            pltpu.VMEM((2, devices) + tile, F32),
+            pltpu.VMEM((KV_HEADS, chips, 2) + tile, F32),
+        ]
+        + [per_head] * 6
+        + [
+            pltpu.VMEM((devices, 8, HEAD_DIM), F32),
+            pltpu.VMEM((KV_HEADS, 8, HEAD_DIM), F32),
+            pltpu.VMEM((devices, 8, HEAD_DIM), F32),
+            pltpu.VMEM((dps, 8, HEAD_DIM), F32),
+        ]
+        + [dma(step) for step in steps],
+        compiler_params=pltpu.CompilerParams(
+            collective_id=0, has_side_effects=True, vmem_limit_bytes=52 * 2**20
+        ),
+    )(queries[0], out_grad[0], key_states[0], value_states[0], sink_tile)
+    return query_grad[None], key_grad[None], value_grad[None], sink_sum[:GROUP, 0]
+
+
+def shards(queries, key_states, value_states, sink_logit, out_grad, block_table):
+    devices = lax.axis_size("seq")
+    dense = queries.shape[1] == BLOCK and devices == KB and devices == KV_HEADS
+    part = dense_shards if dense else sparse_shards
+    return part(queries, key_states, value_states, sink_logit, out_grad, block_table)
+
+
 def solution(mesh):
     in_specs = (
         P("dp", "seq", None),

time: 410 us -> 84 us (0.20); the launches traced: 404 us -> 83.8 us
  other arithmetic: 174 us -> 0 us
  local copies, waits for them, and re-layouts: 104 us -> 6.94 us
  Pallas kernels: 0 us -> 76.2 us
  matrix products: 46.2 us -> 0 us
  starting transfers between devices: 29.9 us -> 0 us
  waiting for transfers between devices: 28.2 us -> 0 us
  blocking collectives: 10.4 us -> 0 us
  loops' own time: 9.54 us -> 0 us
    unnamed x6 -> x0, other arithmetic: 99.6 us -> none
    pallas_call x0 -> x1, Pallas kernels: none -> 76.2 us  [dense_shards(): pl.pallas_call(dense_kernel, in_specs=[vmem] * 5, out_specs=[vmem] * 4, o...]
    scatter-add x4 -> x0, other arithmetic: 68.1 us -> none  [the longest x2 34 us: advance(): value_acc.at[flat_table]]
    dot_general x12 -> x0, matrix products: 46.2 us -> none  [the longest x2 13.6 us: advance(): jnp.einsum('hgqk,gqhd->hgkd', dscores, query_group, preferred_element_typ...]
    unnamed x27 -> x9, local copies, waits for them, and re-layouts: 40.7 us -> 6.24 us
    broadcast_in_dim x4 -> x0, local copies, waits for them, and re-layouts: 33.9 us -> none  [the longest x2 17 us: shards(): jnp.repeat(value_states.reshape(1, tokens_here, KV_HEADS, 1, HEAD_DIM), g...]
    all_to_all x6 -> x0, starting transfers between devices: 29.9 us -> none  [the longest x1 6.33 us: shards(): lax.all_to_all(key_wide, 'seq', split_axis=2, concat_axis=1, tiled=True)]
    all_to_all x6 -> x0, waiting for transfers between devices: 28.2 us -> none  [the longest x1 14.3 us: shards(): lax.all_to_all(out_grad, 'seq', split_axis=2, concat_axis=1, tiled=True)]
  transfers between devices with their start and end apart: 6 -> 0, of which waited for: 3 -> 0; matrix products, arithmetic and copies ran while one was open for 33% -> 0% of each run, Pallas kernels for 0% -> 0%
where the time goes in v1:
time: 84 us; the launch traced here: 83.8 us
  Pallas kernels  76.2 us (91%)
  local copies, waits for them, and re-layouts  6.94 us (8%)
    pallas_call x1, Pallas kernels, dense_shards(): pl.pallas_call(dense_kernel, in_specs=[vmem] * 5, out_specs=[vmem] * 4, o...  76.2 us
    unnamed x9, local copies, waits for them, and re-layouts  6.24 us

profile of v1, /device:TPU:0, one launch (start us, length us, event | category | flops | bytes accessed | tf_op | source)
XLA Modules:
  0.0 83.8 jit_solution(15317980240154240712)
XLA Ops:
  0.6 0.0 copy-start.2
  0.6 0.6 copy-done.2
  1.3 0.1 pad.7.sink_ref
  1.4 0.0 copy-start
  1.4 0.9 %copy-done = bf16[1,128,1024]{2,1,0:T(8,128)(2,1)S(1)} copy-done((bf16[1,128,1024]{2,1,0:T(8,128)(2,1)S(1)}, bf16[1,128,1024]{2,1,0:T(8,128)(2,1)}, u32[]{:S(2)}) %copy-start) | copy-done | bytes 262168
  2.3 0.0 copy-start.1
  2.3 0.9 %copy-done.1 = bf16[1,128,1024]{2,1,0:T(8,128)(2,1)S(1)} copy-done((bf16[1,128,1024]{2,1,0:T(8,128)(2,1)S(1)}, bf16[1,128,1024]{2,1,0:T(8,128)(2,1)}, u32[]{:S(2)}) %copy-start.1) | copy-done | bytes 262168
  3.3 76.2 %shard_map.84 = (bf16[128,4096]{1,0:T(8,128)(2,1)}, bf16[128,1024]{1,0:T(8,128)(2,1)S(1)}, bf16[128,1024]{1,0:T(8,128)(2,1)S(1)}, f32[8,128]{1,0:T(8,128)S(1)}) custom-call(bf16[128,4096]{1,0:T(8,128)(2,1)} %bitcast.11, bf16[128,4096]{1,0:T(8,128)(2,1)} %bitcast.12, bf16[128,1024]{1,0:T(8,128)(2,1)S(1)} %bitcast.7, bf16[128,1024]{1,0:T(8,128)(2,1)S(1)} %bitcast.8, ...), custom_call_target="tpu_custom_call" | custom-call | tf_op jit(solution)/shard_map/pallas_call | solution.py:463
  79.4 0.6 slice_reduce_fusion
  80.1 2.3 %copy.12 = bf16[1,128,4096]{2,1,0:T(8,128)(2,1)} copy(bf16[1,128,4096]{2,1,0:T(8,128)(2,1)} %bitcast.13) | data formatting | bytes 2097152
  82.4 0.7 copy.13
  83.1 0.7 copy.14
  (1 shorter events, 0.0 us)
Async XLA Ops:
  0.6 0.7 copy-start.2
  1.4 0.9 %copy-start = (bf16[1,128,1024]{2,1,0:T(8,128)(2,1)S(1)}, bf16[1,128,1024]{2,1,0:T(8,128)(2,1)}, u32[]{:S(2)}) copy-start(bf16[1,128,1024]{2,1,0:T(8,128)(2,1)} %param.7) | copy-start | bytes 786436
  2.3 0.9 %copy-start.1 = (bf16[1,128,1024]{2,1,0:T(8,128)(2,1)S(1)}, bf16[1,128,1024]{2,1,0:T(8,128)(2,1)}, u32[]{:S(2)}) copy-start(bf16[1,128,1024]{2,1,0:T(8,128)(2,1)} %param.8) | copy-start | bytes 786436

commit v2 on v1

--- a/solution.py
+++ b/solution.py
@@ -144,9 +144,9 @@
     q_ref, g_ref, k_ref, v_ref, sink_ref,
     dq_ref, dk_ref, dv_ref, ds_ref,
     kv_all, acc, part, pair_out, pair_in, right_out, right_in, left_out, left_in,
-    sink_all, sink_part, sink_in, sink_dp,
+    sink_all, sink_part, sink_in, sink_dp, q_here, g_here,
     right_s, right_r, left_s, left_r, sib_s, sib_r, pair_s, pair_r,
-    sumr_s, sumr_r, suml_s, suml_r, logit_s, logit_r, sg_s, sg_r, dp_s, dp_r,
+    sumr_s, sumr_r, suml_s, suml_r, logit_s, logit_r, sg_s, sg_r, dp_s, dp_r, load_s, rows_s,
 ):
     devices = lax.axis_size("seq")
     chips = devices // 2
@@ -220,15 +220,30 @@
             device_id_type=pl.DeviceIdType.MESH,
         )
 
+    def load(which, h):
+        ref = (k_ref, v_ref)[which]
+        cut = pl.ds(pl.multiple_of(h * HEAD_DIM, HEAD_DIM), HEAD_DIM)
+        return pltpu.make_async_copy(ref.at[:, cut], kv_all.at[which, h, me], load_s.at[which, h])
+
+    rows = (
+        pltpu.make_async_copy(q_ref, q_here, rows_s.at[0]),
+        pltpu.make_async_copy(g_ref, g_here, rows_s.at[1]),
+    )
     for h in range(KV_HEADS):
-        cut = slice(h * HEAD_DIM, (h + 1) * HEAD_DIM)
-        kv_all[0, h, me] = k_ref[:, cut]
-        kv_all[1, h, me] = v_ref[:, cut]
-    sink_all[me] = sink_ref[...]
+        for which in range(2):
+            load(which, h).start()
+    for copy in rows:
+        copy.start()
+    sink_all[me] = jnp.zeros_like(sink_all[me])
+    for j in range(GROUP):
+        sink_all[me, j : j + 1, :] = jnp.full((1, HEAD_DIM), sink_ref[j], F32)
     sink_part[...] = jnp.zeros_like(sink_part)
     pl.semaphore_wait(barrier, devices - 1 + dps - 1)
 
     def send_own(h):
+        for which in range(2):
+            load(which, h).wait()
+
         @pl.when(chip < last)
         def _():
             go_right(h, 0, chip).start()
@@ -242,9 +257,12 @@
     send_own(0)
     for i in range(1, devices):
         logit(i, me).start()
-    send_own(1)
-    for i in range(1, devices):
-        logit(i, lax.rem(me - i + devices, devices)).wait_recv()
+
+    def ready_to_compute():
+        for copy in rows:
+            copy.wait()
+        for i in range(1, devices):
+            logit(i, lax.rem(me - i + devices, devices)).wait_recv()
 
     def hand_on(h, k):
         @pl.when(chip >= k)
@@ -269,31 +287,32 @@
 
             go_across(h, chip + k, lane).start()
 
-    def compute(h):
-        for z in range(chips):
-            go_across(h, z, 1 - lane).wait_recv()
+    def compute(h, half):
+        if half == 0:
+            for z in range(chips):
+                go_across(h, z, 1 - lane).wait_recv()
         keys = kv_all[0, h].reshape(devices * here, HEAD_DIM)
         values = kv_all[1, h].reshape(devices * here, HEAD_DIM)
-        key_sum = value_sum = None
-        for half in range(2):
-            heads = range(half * GROUP // 2, (half + 1) * GROUP // 2)
-            cuts = [
-                pl.ds(pl.multiple_of(h * wide + j * HEAD_DIM, HEAD_DIM), HEAD_DIM) for j in heads
-            ]
-            queries = jnp.concatenate([q_ref[:, cut] for cut in cuts], 0)
-            grads = jnp.concatenate([g_ref[:, cut] for cut in cuts], 0)
-            sink_row = jnp.concatenate([sink_all[h, j : j + 1, :] for j in heads], 1)
-            key_terms, value_terms, query_terms, sink_terms = group_terms(
-                keys, values, queries, grads, sink_row
-            )
-            key_sum = key_terms if key_sum is None else key_sum + key_terms
-            value_sum = value_terms if value_sum is None else value_sum + value_terms
-            for i, j in enumerate(heads):
-                span = slice(i * here, (i + 1) * here)
-                dq_ref[:, cuts[i]] = query_terms[span].astype(BF16)
-                sink_part[h, j : j + 1, :] = sink_terms[:, span]
-        acc[0] = (key_sum * SCALE).reshape(devices, here, HEAD_DIM)
-        acc[1] = value_sum.reshape(devices, here, HEAD_DIM)
+        heads = range(half * GROUP // 2, (half + 1) * GROUP // 2)
+        cuts = [pl.ds(pl.multiple_of(h * wide + j * HEAD_DIM, HEAD_DIM), HEAD_DIM) for j in heads]
+        queries = jnp.concatenate([q_here[:, cut] for cut in cuts], 0)
+        grads = jnp.concatenate([g_here[:, cut] for cut in cuts], 0)
+        sink_row = jnp.concatenate([sink_all[h, j : j + 1, :] for j in heads], 1)
+        key_terms, value_terms, query_terms, sink_terms = group_terms(
+            keys, values, queries, grads, sink_row
+        )
+        for i, j in enumerate(heads):
+            span = slice(i * here, (i + 1) * here)
+            dq_ref[:, cuts[i]] = query_terms[span].astype(BF16)
+            sink_part[h, j : j + 1, :] = sink_terms[:, span]
+        key_terms = (key_terms * SCALE).reshape(devices, here, HEAD_DIM)
+        value_terms = value_terms.reshape(devices, here, HEAD_DIM)
+        if half == 0:
+            acc[0] = key_terms
+            acc[1] = value_terms
+            return
+        acc[0] = acc[0] + key_terms
+        acc[1] = acc[1] + value_terms
         for d in range(chips):
             pair_out[h, d] = acc[:, 2 * d + 1 - lane].astype(BF16)
         go_pair(h).start()
@@ -376,7 +395,7 @@
 
     compute_at = chips
     pair_at = compute_at + 1
-    finish_at = pair_at + last
+    finish_at = pair_at + 2 * last
 
     def tick(t, carry):
         def at(h, step, also=None):
@@ -386,19 +405,18 @@
             def _():
                 step(h)
 
-        at(t + 2, send_own)
-        for k in range(1, chips):
-            at(t - k, lambda h: hand_on(h, k))
+        pl.when(t == compute_at)(ready_to_compute)
+        at(t - compute_at, lambda h: compute(h, 0))
         at(t - pair_at, pair_sum)
         at(t - pair_at - chip, pass_right, chip < last)
+        at(t - 3, lambda h: hand_on(h, 3))
+        at(t - compute_at, lambda h: compute(h, 1))
+        at(t - 2, lambda h: hand_on(h, 2))
         at(t - pair_at - (last - chip), pass_left, chip > 0)
-        at(t - compute_at, compute)
+        at(t - 1, lambda h: hand_on(h, 1))
+        at(t + 1, send_own)
         at(t - finish_at, finish)
-
-        @pl.when(t == compute_at + KV_HEADS + 1)
-        def _():
-            sink_sum()
-
+        pl.when(t == compute_at + KV_HEADS + 1)(sink_sum)
         return carry
 
     lax.fori_loop(0, finish_at + KV_HEADS, tick, 0)
@@ -453,16 +471,16 @@
     dps = lax.axis_size("dp")
     here = queries.shape[1]
     tile = (here, HEAD_DIM)
-    sink_tile = jnp.pad(jnp.broadcast_to(sink_logit[:, None], (GROUP, HEAD_DIM)), ((0, 8 - GROUP), (0, 0)))
     dma = pltpu.SemaphoreType.DMA
     vmem = pl.BlockSpec(memory_space=pltpu.VMEM)
     flat = KV_HEADS * HEAD_DIM
     steps = [(KV_HEADS, chips - 1)] * 4 + [(KV_HEADS, chips)] * 2 + [(KV_HEADS,)] * 2
-    steps += [(KV_HEADS, chips)] * 4 + [(devices,)] * 4 + [(dps,)] * 2
+    steps += [(KV_HEADS, chips)] * 4 + [(devices,)] * 4 + [(dps,)] * 2 + [(2, KV_HEADS), (2,)]
     per_head = pltpu.VMEM((KV_HEADS, chips, 2) + tile, BF16)
     query_grad, key_grad, value_grad, sink_sum = pl.pallas_call(
         dense_kernel,
-        in_specs=[vmem] * 5,
+        in_specs=[pl.BlockSpec(memory_space=pltpu.HBM)] * 4
+        + [pl.BlockSpec(memory_space=pltpu.SMEM)],
         out_specs=[vmem] * 4,
         out_shape=[
             jax.ShapeDtypeStruct((here, HEADS * HEAD_DIM), BF16),
@@ -481,12 +499,14 @@
             pltpu.VMEM((KV_HEADS, 8, HEAD_DIM), F32),
             pltpu.VMEM((devices, 8, HEAD_DIM), F32),
             pltpu.VMEM((dps, 8, HEAD_DIM), F32),
+            pltpu.VMEM((here, HEADS * HEAD_DIM), BF16),
+            pltpu.VMEM((here, HEADS * HEAD_DIM), BF16),
         ]
         + [dma(step) for step in steps],
         compiler_params=pltpu.CompilerParams(
-            collective_id=0, has_side_effects=True, vmem_limit_bytes=52 * 2**20
+            collective_id=0, has_side_effects=True, vmem_limit_bytes=62 * 2**20
         ),
-    )(queries[0], out_grad[0], key_states[0], value_states[0], sink_tile)
+    )(queries[0], out_grad[0], key_states[0], value_states[0], sink_logit)
     return query_grad[None], key_grad[None], value_grad[None], sink_sum[:GROUP, 0]
 
 

time: 84 us -> 79.9 us (0.951)
  Pallas kernels: 76.2 us -> 73.6 us
  local copies, waits for them, and re-layouts: 6.94 us -> 5.37 us
    pallas_call x1, Pallas kernels: 76.2 us -> 73.6 us  [dense_shards(): pl.pallas_call(dense_kernel, in_specs=[pl.BlockSpec(memory_space=pltpu.HB...]
    unnamed x9, local copies, waits for them, and re-layouts: 6.24 us -> 4.74 us
where the time goes in v2:
time: 79.9 us; the launch traced here: 79.7 us
  Pallas kernels  73.6 us (92%)
  local copies, waits for them, and re-layouts  5.37 us (7%)
    pallas_call x1, Pallas kernels, dense_shards(): pl.pallas_call(dense_kernel, in_specs=[pl.BlockSpec(memory_space=pltpu.HB...  73.6 us
    unnamed x9, local copies, waits for them, and re-layouts  4.74 us

profile of v2, /device:TPU:0, one launch (start us, length us, event | category | flops | bytes accessed | tf_op | source)
XLA Modules:
  0.0 79.7 jit_solution(4198767562318777818)
XLA Ops:
  0.6 73.6 %shard_map.84 = (bf16[128,4096]{1,0:T(8,128)(2,1)}, bf16[128,1024]{1,0:T(8,128)(2,1)}, bf16[128,1024]{1,0:T(8,128)(2,1)}, f32[8,128]{1,0:T(8,128)}) custom-call(bf16[128,4096]{1,0:T(8,128)(2,1)} %bitcast.7, bf16[128,4096]{1,0:T(8,128)(2,1)} %bitcast.8, bf16[128,1024]{1,0:T(8,128)(2,1)} %bitcast.12, bf16[128,1024]{1,0:T(8,128)(2,1)} %bitcast.13, f32[4]{0:T(128)} %sink_ref.1), custom_call_target="tpu_custom_call" | custom-call | tf_op jit(solution)/shard_map/pallas_call | solution.py:480
  74.3 0.0 copy-start.2
  74.3 0.7 copy-done.2
  75.0 0.6 slice_reduce_fusion
  75.6 0.0 copy-start.1
  75.6 2.3 %copy.12 = bf16[1,128,4096]{2,1,0:T(8,128)(2,1)} copy(bf16[1,128,4096]{2,1,0:T(8,128)(2,1)} %bitcast.9) | data formatting | bytes 2097152
  77.9 0.0 copy-done.1
  77.9 0.0 copy-start
  77.9 0.7 copy.13
  78.6 0.3 copy-done
  79.0 0.7 copy.14
Async XLA Ops:
  74.3 0.7 copy-start.2
  75.6 2.3 %copy-start.1 = (bf16[128,1024]{1,0:T(8,128)(2,1)S(1)}, bf16[128,1024]{1,0:T(8,128)(2,1)}, u32[]{:S(2)}) copy-start(bf16[128,1024]{1,0:T(8,128)(2,1)} %get-tuple-element.9) | copy-start | bytes 786436
  77.9 1.0 %copy-start = (bf16[128,1024]{1,0:T(8,128)(2,1)S(1)}, bf16[128,1024]{1,0:T(8,128)(2,1)}, u32[]{:S(2)}) copy-start(bf16[128,1024]{1,0:T(8,128)(2,1)} %get-tuple-element.10) | copy-start | bytes 786436

commit v3 on v2

--- a/solution.py
+++ b/solution.py
@@ -119,15 +119,16 @@
 BF16 = jnp.bfloat16
 GROUP = HEADS // KV_HEADS
 SCALE = HEAD_DIM ** (-0.5)
+LOG2E = 1.4426950408889634
 
 
 def group_terms(keys, values, queries, grads, sink_row):
     nt = (((1,), (1,)), ((), ()))
     tn = (((0,), (0,)), ((), ()))
-    scores = lax.dot_general(keys, queries, nt, preferred_element_type=F32) * SCALE
+    scores = lax.dot_general(keys, queries, nt, preferred_element_type=F32)
     dprobs = lax.dot_general(values, grads, nt, preferred_element_type=F32)
-    top = jnp.maximum(jnp.max(scores, 0, keepdims=True), sink_row)
-    weights = jnp.exp(scores - top)
+    top = jnp.maximum(jnp.max(scores, 0, keepdims=True) * SCALE, sink_row)
+    weights = jnp.exp2(scores * (SCALE * LOG2E) - top * LOG2E)
     sink_weight = jnp.exp(sink_row - top)
     inverse = 1.0 / (jnp.sum(weights, 0, keepdims=True) + sink_weight)
     probs = weights * inverse
@@ -144,9 +145,9 @@
     q_ref, g_ref, k_ref, v_ref, sink_ref,
     dq_ref, dk_ref, dv_ref, ds_ref,
     kv_all, acc, part, pair_out, pair_in, right_out, right_in, left_out, left_in,
-    sink_all, sink_part, sink_in, sink_dp, q_here, g_here,
+    sink_all, sink_part, sink_in, sink_dp, q_here, g_here, dq_here, dk_here, dv_here,
     right_s, right_r, left_s, left_r, sib_s, sib_r, pair_s, pair_r,
-    sumr_s, sumr_r, suml_s, suml_r, logit_s, logit_r, sg_s, sg_r, dp_s, dp_r, load_s, rows_s,
+    sumr_s, sumr_r, suml_s, suml_r, logit_s, logit_r, sg_s, sg_r, dp_s, dp_r, load_s, rows_s, leave_s,
 ):
     devices = lax.axis_size("seq")
     chips = devices // 2
@@ -240,6 +241,12 @@
     sink_part[...] = jnp.zeros_like(sink_part)
     pl.semaphore_wait(barrier, devices - 1 + dps - 1)
 
+    def leave(which, h):
+        held, out = ((dq_here, dq_ref), (dk_here, dk_ref), (dv_here, dv_ref))[which]
+        size = wide if which == 0 else HEAD_DIM
+        cut = pl.ds(pl.multiple_of(h * size, size), size)
+        return pltpu.make_async_copy(held.at[:, cut], out.at[:, cut], leave_s.at[which, h])
+
     def send_own(h):
         for which in range(2):
             load(which, h).wait()
@@ -287,35 +294,33 @@
 
             go_across(h, chip + k, lane).start()
 
-    def compute(h, half):
-        if half == 0:
-            for z in range(chips):
-                go_across(h, z, 1 - lane).wait_recv()
+    def compute(h):
+        for z in range(chips):
+            go_across(h, z, 1 - lane).wait_recv()
         keys = kv_all[0, h].reshape(devices * here, HEAD_DIM)
         values = kv_all[1, h].reshape(devices * here, HEAD_DIM)
-        heads = range(half * GROUP // 2, (half + 1) * GROUP // 2)
-        cuts = [pl.ds(pl.multiple_of(h * wide + j * HEAD_DIM, HEAD_DIM), HEAD_DIM) for j in heads]
-        queries = jnp.concatenate([q_here[:, cut] for cut in cuts], 0)
-        grads = jnp.concatenate([g_here[:, cut] for cut in cuts], 0)
-        sink_row = jnp.concatenate([sink_all[h, j : j + 1, :] for j in heads], 1)
-        key_terms, value_terms, query_terms, sink_terms = group_terms(
-            keys, values, queries, grads, sink_row
-        )
-        for i, j in enumerate(heads):
-            span = slice(i * here, (i + 1) * here)
-            dq_ref[:, cuts[i]] = query_terms[span].astype(BF16)
-            sink_part[h, j : j + 1, :] = sink_terms[:, span]
-        key_terms = (key_terms * SCALE).reshape(devices, here, HEAD_DIM)
-        value_terms = value_terms.reshape(devices, here, HEAD_DIM)
-        if half == 0:
-            acc[0] = key_terms
-            acc[1] = value_terms
-            return
-        acc[0] = acc[0] + key_terms
-        acc[1] = acc[1] + value_terms
+        key_sum = value_sum = None
+        for half in range(2):
+            heads = range(half * GROUP // 2, (half + 1) * GROUP // 2)
+            cuts = [pl.ds(pl.multiple_of(h * wide + j * HEAD_DIM, HEAD_DIM), HEAD_DIM) for j in heads]
+            queries = jnp.concatenate([q_here[:, cut] for cut in cuts], 0)
+            grads = jnp.concatenate([g_here[:, cut] for cut in cuts], 0)
+            sink_row = jnp.concatenate([sink_all[h, j : j + 1, :] for j in heads], 1)
+            key_terms, value_terms, query_terms, sink_terms = group_terms(
+                keys, values, queries, grads, sink_row
+            )
+            for i, j in enumerate(heads):
+                span = slice(i * here, (i + 1) * here)
+                dq_here[:, cuts[i]] = query_terms[span].astype(BF16)
+                sink_part[h, j : j + 1, :] = sink_terms[:, span]
+            key_sum = key_terms if half == 0 else key_sum + key_terms
+            value_sum = value_terms if half == 0 else value_sum + value_terms
+        acc[0] = (key_sum * SCALE).reshape(devices, here, HEAD_DIM)
+        acc[1] = value_sum.reshape(devices, here, HEAD_DIM)
         for d in range(chips):
             pair_out[h, d] = acc[:, 2 * d + 1 - lane].astype(BF16)
         go_pair(h).start()
+        leave(0, h).start()
         for d in range(chips):
             part[h, d] = acc[:, 2 * d + lane]
 
@@ -376,8 +381,10 @@
             part[h, chip] = part[h, chip] + left_in[h, chip].astype(F32)
 
         cut = pl.ds(pl.multiple_of(h * HEAD_DIM, HEAD_DIM), HEAD_DIM)
-        dk_ref[:, cut] = part[h, chip, 0].astype(BF16)
-        dv_ref[:, cut] = part[h, chip, 1].astype(BF16)
+        dk_here[:, cut] = part[h, chip, 0].astype(BF16)
+        dv_here[:, cut] = part[h, chip, 1].astype(BF16)
+        leave(1, h).start()
+        leave(2, h).start()
 
     def sink_sum():
         for p in range(devices):
@@ -395,7 +402,7 @@
 
     compute_at = chips
     pair_at = compute_at + 1
-    finish_at = pair_at + 2 * last
+    finish_at = pair_at + 2 * last - 1
 
     def tick(t, carry):
         def at(h, step, also=None):
@@ -406,13 +413,12 @@
                 step(h)
 
         pl.when(t == compute_at)(ready_to_compute)
-        at(t - compute_at, lambda h: compute(h, 0))
+        at(t - compute_at, compute)
         at(t - pair_at, pair_sum)
+        at(t - 3, lambda h: hand_on(h, 3))
         at(t - pair_at - chip, pass_right, chip < last)
-        at(t - 3, lambda h: hand_on(h, 3))
-        at(t - compute_at, lambda h: compute(h, 1))
+        at(t - pair_at - (last - chip), pass_left, chip > 0)
         at(t - 2, lambda h: hand_on(h, 2))
-        at(t - pair_at - (last - chip), pass_left, chip > 0)
         at(t - 1, lambda h: hand_on(h, 1))
         at(t + 1, send_own)
         at(t - finish_at, finish)
@@ -426,7 +432,8 @@
     total = sink_dp[0]
     for i in range(1, dps):
         total = total + sink_dp[i]
-    ds_ref[...] = jnp.broadcast_to(jnp.sum(total, 1, keepdims=True), ds_ref.shape)
+    for j in range(GROUP):
+        ds_ref[j] = jnp.sum(total[j : j + 1])
 
     def drain(h, carry):
         for k in range(last):
@@ -442,6 +449,8 @@
         for z in range(chips):
             go_across(h, z, lane).wait_send()
         go_pair(h).wait_send()
+        for which in range(3):
+            leave(which, h).wait()
         for d in range(chips):
 
             @pl.when(d > chip)
@@ -463,6 +472,20 @@
         logit(i, me).wait_send()
     for i in range(1, dps):
         across_dp(i, my_dp).wait_send()
+
+
+def place_kernel(*refs):
+    held, out, sems = refs[:4], refs[4:8], refs[8]
+    rows = held[0].shape[0] // 4
+    pairs = [(held[0].at[pl.ds(i * rows, rows)], out[0].at[pl.ds(i * rows, rows)]) for i in range(4)]
+    pairs += [(held[1], out[1]), (held[2], out[2])]
+    copies = [pltpu.make_async_copy(*pair, sems.at[i]) for i, pair in enumerate(pairs)]
+    for copy in copies:
+        copy.start()
+    for j in range(GROUP):
+        out[3][j] = held[3][j]
+    for copy in copies:
+        copy.wait()
 
 
 def dense_shards(queries, key_states, value_states, sink_logit, out_grad, block_table):
@@ -472,22 +495,23 @@
     here = queries.shape[1]
     tile = (here, HEAD_DIM)
     dma = pltpu.SemaphoreType.DMA
-    vmem = pl.BlockSpec(memory_space=pltpu.VMEM)
+    hbm = pl.BlockSpec(memory_space=pltpu.HBM)
+    smem = pl.BlockSpec(memory_space=pltpu.SMEM)
     flat = KV_HEADS * HEAD_DIM
     steps = [(KV_HEADS, chips - 1)] * 4 + [(KV_HEADS, chips)] * 2 + [(KV_HEADS,)] * 2
-    steps += [(KV_HEADS, chips)] * 4 + [(devices,)] * 4 + [(dps,)] * 2 + [(2, KV_HEADS), (2,)]
+    steps += [(KV_HEADS, chips)] * 4 + [(devices,)] * 4 + [(dps,)] * 2 + [(2, KV_HEADS), (2,), (3, KV_HEADS)]
     per_head = pltpu.VMEM((KV_HEADS, chips, 2) + tile, BF16)
-    query_grad, key_grad, value_grad, sink_sum = pl.pallas_call(
+    results = [
+        jax.ShapeDtypeStruct((here, HEADS * HEAD_DIM), BF16),
+        jax.ShapeDtypeStruct((here, flat), BF16),
+        jax.ShapeDtypeStruct((here, flat), BF16),
+        jax.ShapeDtypeStruct((GROUP,), F32),
+    ]
+    held = pl.pallas_call(
         dense_kernel,
-        in_specs=[pl.BlockSpec(memory_space=pltpu.HBM)] * 4
-        + [pl.BlockSpec(memory_space=pltpu.SMEM)],
-        out_specs=[vmem] * 4,
-        out_shape=[
-            jax.ShapeDtypeStruct((here, HEADS * HEAD_DIM), BF16),
-            jax.ShapeDtypeStruct((here, flat), BF16),
-            jax.ShapeDtypeStruct((here, flat), BF16),
-            jax.ShapeDtypeStruct((8, HEAD_DIM), F32),
-        ],
+        in_specs=[hbm] * 4 + [smem],
+        out_specs=[hbm] * 3 + [smem],
+        out_shape=results,
         scratch_shapes=[
             pltpu.VMEM((2, KV_HEADS, devices) + tile, BF16),
             pltpu.VMEM((2, devices) + tile, F32),
@@ -499,15 +523,23 @@
             pltpu.VMEM((KV_HEADS, 8, HEAD_DIM), F32),
             pltpu.VMEM((devices, 8, HEAD_DIM), F32),
             pltpu.VMEM((dps, 8, HEAD_DIM), F32),
-            pltpu.VMEM((here, HEADS * HEAD_DIM), BF16),
-            pltpu.VMEM((here, HEADS * HEAD_DIM), BF16),
         ]
+        + [pltpu.VMEM((here, HEADS * HEAD_DIM), BF16)] * 3
+        + [pltpu.VMEM((here, flat), BF16)] * 2
         + [dma(step) for step in steps],
         compiler_params=pltpu.CompilerParams(
             collective_id=0, has_side_effects=True, vmem_limit_bytes=62 * 2**20
         ),
     )(queries[0], out_grad[0], key_states[0], value_states[0], sink_logit)
-    return query_grad[None], key_grad[None], value_grad[None], sink_sum[:GROUP, 0]
+    query_grad, key_grad, value_grad, sink_grad = pl.pallas_call(
+        place_kernel,
+        in_specs=[hbm] * 3 + [smem],
+        out_specs=[hbm] * 3 + [smem],
+        out_shape=results,
+        scratch_shapes=[dma((6,))],
+        compiler_params=pltpu.CompilerParams(vmem_limit_bytes=62 * 2**20),
+    )(*held)
+    return query_grad[None], key_grad[None], value_grad[None], sink_grad
 
 
 def shards(queries, key_states, value_states, sink_logit, out_grad, block_table):

time: 79.9 us -> 124 us (1.55)
  Pallas kernels: 73.6 us -> 124 us
  local copies, waits for them, and re-layouts: 5.37 us -> 0 us
    pallas_call x1 -> x2, Pallas kernels: 73.6 us -> 124 us  [the longest x1 73.6 us: dense_shards(): pl.pallas_call(dense_kernel, in_specs=[hbm] * 4 + [smem], out_specs=[hbm]...]
    unnamed x9 -> x0, local copies, waits for them, and re-layouts: 4.74 us -> none
where the time goes in v3:
time: 124 us
  Pallas kernels  124 us (100%)
    pallas_call x1, Pallas kernels, dense_shards(): pl.pallas_call(dense_kernel, in_specs=[hbm] * 4 + [smem], out_specs=[hbm]...  73.6 us
    pallas_call x1, Pallas kernels, dense_shards(): pl.pallas_call(place_kernel, in_specs=[hbm] * 3 + [smem], out_specs=[hbm]...  50 us

profile of v3, /device:TPU:0, one launch (start us, length us, event | category | flops | bytes accessed | tf_op | source)
XLA Modules:
  0.0 124.2 jit_solution(4766356059365135910)
XLA Ops:
  0.6 73.6 %shard_map.84 = (bf16[128,4096]{1,0:T(8,128)(2,1)}, bf16[128,1024]{1,0:T(8,128)(2,1)}, bf16[128,1024]{1,0:T(8,128)(2,1)}, f32[4]{0:T(128)}) custom-call(bf16[128,4096]{1,0:T(8,128)(2,1)} %bitcast.7, bf16[128,4096]{1,0:T(8,128)(2,1)} %bitcast.8, bf16[128,1024]{1,0:T(8,128)(2,1)} %bitcast.9, bf16[128,1024]{1,0:T(8,128)(2,1)} %bitcast.10, f32[4]{0:T(128)} %sink_ref.1), custom_call_target="tpu_custom_call" | custom-call | tf_op jit(solution)/shard_map/pallas_call | solution.py:510
  74.2 50.0 %shard_map.85 = (bf16[128,4096]{1,0:T(8,128)(2,1)}, bf16[128,1024]{1,0:T(8,128)(2,1)}, bf16[128,1024]{1,0:T(8,128)(2,1)}, f32[4]{0:T(128)}) custom-call(bf16[128,4096]{1,0:T(8,128)(2,1)} %get-tuple-element.12.refs_0_, bf16[128,1024]{1,0:T(8,128)(2,1)} %get-tuple-element.13.refs_1_, bf16[128,1024]{1,0:T(8,128)(2,1)} %get-tuple-element.14.refs_2_, ...), custom_call_target="tpu_custom_call" | custom-call | tf_op jit(solution)/shard_map/pallas_call | solution.py:534

commit v4 on v3

--- a/solution.py
+++ b/solution.py
@@ -476,10 +476,7 @@
 
 def place_kernel(*refs):
     held, out, sems = refs[:4], refs[4:8], refs[8]
-    rows = held[0].shape[0] // 4
-    pairs = [(held[0].at[pl.ds(i * rows, rows)], out[0].at[pl.ds(i * rows, rows)]) for i in range(4)]
-    pairs += [(held[1], out[1]), (held[2], out[2])]
-    copies = [pltpu.make_async_copy(*pair, sems.at[i]) for i, pair in enumerate(pairs)]
+    copies = [pltpu.make_async_copy(held[i], out[i], sems.at[i]) for i in range(3)]
     for copy in copies:
         copy.start()
     for j in range(GROUP):
@@ -533,10 +530,10 @@
     )(queries[0], out_grad[0], key_states[0], value_states[0], sink_logit)
     query_grad, key_grad, value_grad, sink_grad = pl.pallas_call(
         place_kernel,
-        in_specs=[hbm] * 3 + [smem],
+        in_specs=[pl.BlockSpec(memory_space=pltpu.VMEM)] * 3 + [smem],
         out_specs=[hbm] * 3 + [smem],
         out_shape=results,
-        scratch_shapes=[dma((6,))],
+        scratch_shapes=[dma((3,))],
         compiler_params=pltpu.CompilerParams(vmem_limit_bytes=62 * 2**20),
     )(*held)
     return query_grad[None], key_grad[None], value_grad[None], sink_grad

time: 124 us -> 77.4 us (0.62)
  Pallas kernels: 124 us -> 76.6 us
    pallas_call x1, Pallas kernels: 50 us -> 3.03 us  [dense_shards(): pl.pallas_call(place_kernel, in_specs=[pl.BlockSpec(memory_space=pltpu.VM...]
where the time goes in v4:
time: 77.4 us; the launch traced here: 77.2 us
  Pallas kernels  76.6 us (99%)
    pallas_call x1, Pallas kernels, dense_shards(): pl.pallas_call(dense_kernel, in_specs=[hbm] * 4 + [smem], out_specs=[hbm]...  73.6 us
    pallas_call x1, Pallas kernels, dense_shards(): pl.pallas_call(place_kernel, in_specs=[pl.BlockSpec(memory_space=pltpu.VM...  3.03 us

profile of v4, /device:TPU:0, one launch (start us, length us, event | category | flops | bytes accessed | tf_op | source)
XLA Modules:
  0.0 77.2 jit_solution(12781648854587359888)
XLA Ops:
  0.6 73.6 %shard_map.84 = (bf16[128,4096]{1,0:T(8,128)(2,1)}, bf16[128,1024]{1,0:T(8,128)(2,1)}, bf16[128,1024]{1,0:T(8,128)(2,1)}, f32[4]{0:T(128)}) custom-call(bf16[128,4096]{1,0:T(8,128)(2,1)} %bitcast.7, bf16[128,4096]{1,0:T(8,128)(2,1)} %bitcast.8, bf16[128,1024]{1,0:T(8,128)(2,1)} %bitcast.9, bf16[128,1024]{1,0:T(8,128)(2,1)} %bitcast.10, f32[4]{0:T(128)} %sink_ref.1), custom_call_target="tpu_custom_call" | custom-call | tf_op jit(solution)/shard_map/pallas_call | solution.py:507
  74.2 3.0 %shard_map.85 = (bf16[128,4096]{1,0:T(8,128)(2,1)}, bf16[128,1024]{1,0:T(8,128)(2,1)}, bf16[128,1024]{1,0:T(8,128)(2,1)}, f32[4]{0:T(128)}) custom-call(bf16[128,4096]{1,0:T(8,128)(2,1)} %get-tuple-element.12.refs_0_, bf16[128,1024]{1,0:T(8,128)(2,1)} %get-tuple-element.13.refs_1_, bf16[128,1024]{1,0:T(8,128)(2,1)} %get-tuple-element.14.refs_2_, ...), custom_call_target="tpu_custom_call" | custom-call | tf_op jit(solution)/shard_map/pallas_call | solution.py:531

commit v5 on v3

--- a/solution.py
+++ b/solution.py
@@ -1,3 +1,5 @@
+import functools
+
 import jax
 import jax.numpy as jnp
 from jax import lax
@@ -119,6 +121,7 @@
 BF16 = jnp.bfloat16
 GROUP = HEADS // KV_HEADS
 SCALE = HEAD_DIM ** (-0.5)
+AHEAD = 4
 LOG2E = 1.4426950408889634
 
 
@@ -247,21 +250,25 @@
         cut = pl.ds(pl.multiple_of(h * size, size), size)
         return pltpu.make_async_copy(held.at[:, cut], out.at[:, cut], leave_s.at[which, h])
 
-    def send_own(h):
+    def send_right(h):
+        go_right(h, 0, chip).start()
+
+    def send_left(h):
+        go_left(h, 0, chip).start()
+
+    def send_across(h):
+        go_across(h, chip, lane).start()
+
+    far = last - chip
+    right_ahead = 1 + AHEAD * (1 - jnp.minimum(chip, 1))
+    left_ahead = 1 + AHEAD * (1 - jnp.minimum(far, 1))
+    for h in range(KV_HEADS):
         for which in range(2):
             load(which, h).wait()
-
-        @pl.when(chip < last)
-        def _():
-            go_right(h, 0, chip).start()
-
-        @pl.when(chip > 0)
-        def _():
-            go_left(h, 0, chip).start()
-
-        go_across(h, chip, lane).start()
-
-    send_own(0)
+    send_across(0)
+    for h in range(AHEAD + 1):
+        pl.when((chip < last) & (h < right_ahead))(functools.partial(send_right, h))
+        pl.when((chip > 0) & (h < left_ahead))(functools.partial(send_left, h))
     for i in range(1, devices):
         logit(i, me).start()
 
@@ -402,7 +409,7 @@
 
     compute_at = chips
     pair_at = compute_at + 1
-    finish_at = pair_at + 2 * last - 1
+    finish_at = pair_at + 2 * last + 2
 
     def tick(t, carry):
         def at(h, step, also=None):
@@ -413,15 +420,17 @@
                 step(h)
 
         pl.when(t == compute_at)(ready_to_compute)
+        at(t - finish_at, finish)
         at(t - compute_at, compute)
         at(t - pair_at, pair_sum)
         at(t - 3, lambda h: hand_on(h, 3))
-        at(t - pair_at - chip, pass_right, chip < last)
-        at(t - pair_at - (last - chip), pass_left, chip > 0)
+        at(t - pair_at - far - jnp.minimum(far, 1), pass_left, chip > 0)
+        at(t - pair_at - chip - jnp.minimum(chip, 1), pass_right, chip < last)
         at(t - 2, lambda h: hand_on(h, 2))
         at(t - 1, lambda h: hand_on(h, 1))
-        at(t + 1, send_own)
-        at(t - finish_at, finish)
+        at(t + right_ahead, send_right, chip < last)
+        at(t + left_ahead, send_left, chip > 0)
+        at(t + 1, send_across)
         pl.when(t == compute_at + KV_HEADS + 1)(sink_sum)
         return carry
 
@@ -475,16 +484,23 @@
 
 
 def place_kernel(*refs):
-    held, out, sems = refs[:4], refs[4:8], refs[8]
+    held, out, space, come, go = refs[:4], refs[4:8], refs[8:11], refs[11], refs[12]
     rows = held[0].shape[0] // 4
-    pairs = [(held[0].at[pl.ds(i * rows, rows)], out[0].at[pl.ds(i * rows, rows)]) for i in range(4)]
-    pairs += [(held[1], out[1]), (held[2], out[2])]
-    copies = [pltpu.make_async_copy(*pair, sems.at[i]) for i, pair in enumerate(pairs)]
-    for copy in copies:
+    cuts = [(0, pl.ds(i * rows, rows)) for i in range(4)]
+    cuts += [(1, pl.ds(0, 4 * rows)), (2, pl.ds(0, 4 * rows))]
+    loads, stores = [], []
+    for i, (which, cut) in enumerate(cuts):
+        here = space[which].at[cut]
+        loads.append(pltpu.make_async_copy(held[which].at[cut], here, come.at[i]))
+        stores.append(pltpu.make_async_copy(here, out[which].at[cut], go.at[i]))
+    for copy in loads:
         copy.start()
     for j in range(GROUP):
         out[3][j] = held[3][j]
-    for copy in copies:
+    for first, second in zip(loads, stores):
+        first.wait()
+        second.start()
+    for copy in stores:
         copy.wait()
 
 
@@ -536,7 +552,8 @@
         in_specs=[hbm] * 3 + [smem],
         out_specs=[hbm] * 3 + [smem],
         out_shape=results,
-        scratch_shapes=[dma((6,))],
+        scratch_shapes=[pltpu.VMEM(result.shape, BF16) for result in results[:3]]
+        + [dma((6,)), dma((6,))],
         compiler_params=pltpu.CompilerParams(vmem_limit_bytes=62 * 2**20),
     )(*held)
     return query_grad[None], key_grad[None], value_grad[None], sink_grad

time: 124 us -> 74.4 us (0.60)
  Pallas kernels: 124 us -> 73.6 us
    pallas_call x1, Pallas kernels: 50 us -> 3.37 us  [dense_shards(): pl.pallas_call(place_kernel, in_specs=[hbm] * 3 + [smem], out_specs=[hbm]...]
    pallas_call x1, Pallas kernels: 73.6 us -> 70.2 us  [dense_shards(): pl.pallas_call(dense_kernel, in_specs=[hbm] * 4 + [smem], out_specs=[hbm]...]
where the time goes in v5:
time: 74.4 us; the launch traced here: 74.3 us
  Pallas kernels  73.6 us (99%)
    pallas_call x1, Pallas kernels, dense_shards(): pl.pallas_call(dense_kernel, in_specs=[hbm] * 4 + [smem], out_specs=[hbm]...  70.2 us
    pallas_call x1, Pallas kernels, dense_shards(): pl.pallas_call(place_kernel, in_specs=[hbm] * 3 + [smem], out_specs=[hbm]...  3.37 us

profile of v5, /device:TPU:0, one launch (start us, length us, event | category | flops | bytes accessed | tf_op | source)
XLA Modules:
  0.0 74.3 jit_solution(11743232305153680358)
XLA Ops:
  0.6 70.2 %shard_map.84 = (bf16[128,4096]{1,0:T(8,128)(2,1)}, bf16[128,1024]{1,0:T(8,128)(2,1)}, bf16[128,1024]{1,0:T(8,128)(2,1)}, f32[4]{0:T(128)}) custom-call(bf16[128,4096]{1,0:T(8,128)(2,1)} %bitcast.7, bf16[128,4096]{1,0:T(8,128)(2,1)} %bitcast.8, bf16[128,1024]{1,0:T(8,128)(2,1)} %bitcast.9, bf16[128,1024]{1,0:T(8,128)(2,1)} %bitcast.10, f32[4]{0:T(128)} %sink_ref.1), custom_call_target="tpu_custom_call" | custom-call | tf_op jit(solution)/shard_map/pallas_call | solution.py:526
  70.9 3.4 %shard_map.85 = (bf16[128,4096]{1,0:T(8,128)(2,1)}, bf16[128,1024]{1,0:T(8,128)(2,1)}, bf16[128,1024]{1,0:T(8,128)(2,1)}, f32[4]{0:T(128)}) custom-call(bf16[128,4096]{1,0:T(8,128)(2,1)} %get-tuple-element.12.refs_0_, bf16[128,1024]{1,0:T(8,128)(2,1)} %get-tuple-element.13.refs_1_, bf16[128,1024]{1,0:T(8,128)(2,1)} %get-tuple-element.14.refs_2_, ...), custom_call_target="tpu_custom_call" | custom-call | tf_op jit(solution)/shard_map/pallas_call | solution.py:550
